TPU v7x, 128 devices: a whole 4x4x4 slice. The times are simulated.
128 devices in a mesh: gx: 32 (over x, z, core), gz: 4 (over y).
Axes of the slice: x: 4, y: 4, z: 4, core: 2. Of those that a mesh axis runs over, the one named last changes fastest.
Arguments:
- density: bfloat16 [512, 128, 8192], P('gz', None, 'gx'), may hold values from 0 to 1
- tf_color: float32 [3, 8], replicated, may hold values from 0.2 to 1
- tf_extinction: float32 [8], replicated, may hold values from 0.8 to 6
Outputs:
- image: bfloat16 [4, 128, 8192], P(None, 'gz')
All inputs are finite; a program needn't handle non-finite values.
Results may differ from a plain program's by a relative error of at most 0.0004.
Values may be sent and summed in bfloat16 or wider, within the bound.
A program may use at most 192 MiB of HBM per device.

v0:
```python
import jax
import jax.numpy as jnp
from jax import lax
from jax.sharding import PartitionSpec as P


def carried_in(value, axis, join, neutral):
    count, mine = (lax.axis_size(axis), lax.axis_index(axis))
    pieces = lax.all_gather(value, axis)
    running = jnp.full_like(value, 0) + jnp.asarray(neutral, value.dtype)

    def step(position, running):
        longer = join(running, pieces[position])
        return jnp.where(position < mine, longer, running)

    return lax.fori_loop(0, count - 1, step, running)


def with_halo(block, sides, width):
    for axis, dim in sides:
        count = lax.axis_size(axis)
        forward = [(i, i + 1) for i in range(count - 1)]
        backward = [(target, source) for source, target in forward]
        low = lax.ppermute(
            lax.slice_in_dim(block, block.shape[dim] - width, None, axis=dim), axis, forward
        )
        high = lax.ppermute(lax.slice_in_dim(block, 0, width, axis=dim), axis, backward)
        block = jnp.concatenate([low, block, high], axis=dim)
    return block


def shade_and_color(block, tf_color, tf_extinction):
    middle = block[:, :, 1:-1]
    slope_cols = 4.0 * (block[:, :, 2:] - block[:, :, :-2])
    padded_rows = jnp.pad(middle, ((0, 0), (1, 1), (0, 0)))
    slope_rows = 4.0 * (padded_rows[:, 2:, :] - padded_rows[:, :-2, :])
    shading = 0.5 + 0.5 * (0.6 * slope_cols + 0.8 * slope_rows) / jnp.sqrt(
        1.0 + slope_cols * slope_cols + slope_rows * slope_rows
    )
    levels = middle * (tf_extinction.shape[0] - 1)
    colors = [jnp.zeros_like(middle) for channel in range(3)]
    extinct = jnp.zeros_like(middle)
    for knot in range(tf_extinction.shape[0]):
        tent_weight = jnp.maximum(0.0, 1.0 - jnp.abs(levels - knot))
        colors = [colors[channel] + tent_weight * tf_color[channel, knot] for channel in range(3)]
        extinct = extinct + tent_weight * tf_extinction[knot]
    return (shading, colors, extinct)


def brick_strip(shading, colors, extinct, spacing):
    optical = extinct * spacing
    running = jnp.cumsum(optical, axis=0)
    emitted = jnp.exp(-(running - optical)) - jnp.exp(-running)
    lighted = emitted * shading
    planes = [jnp.sum(lighted * colors[channel], axis=0) for channel in range(3)]
    planes.append(1.0 - jnp.exp(-running[-1]))
    return jnp.stack(planes)


def multiply_terms(earlier, later):
    return earlier * later


def composite(strips):
    clearance = 1.0 - strips[3]
    ahead = carried_in(clearance, "gz", multiply_terms, jnp.ones_like(clearance))
    return lax.psum_scatter(strips * ahead[None], "gz", scatter_dimension=1, tiled=True)


def on_device(density, tf_color, tf_extinction):
    spacing = 1.0 / (density.shape[0] * lax.axis_size("gz"))
    edges = jnp.stack([density[:, :, 0], density[:, :, -1]])
    widened = with_halo(edges, (("gx", 0),), 1)
    padded = jnp.concatenate([widened[0][:, :, None], density, widened[3][:, :, None]], axis=2)
    shading, colors, extinct = shade_and_color(padded.astype(jnp.float32), tf_color, tf_extinction)
    strips = brick_strip(shading, colors, extinct, spacing)
    finished = composite(strips).astype(jnp.bfloat16)
    return lax.all_gather(finished, "gx", axis=2, tiled=True)


def solution(mesh):
    in_specs = (P("gz", None, "gx"), P(), P())
    out_specs = P(None, "gz", None)
    return jax.shard_map(
        on_device, mesh=mesh, in_specs=in_specs, out_specs=out_specs, check_vma=False
    )
```

profile of v0, /device:TPU:1, one launch (start us, length us, event | category | flops | bytes accessed | tf_op | source)
XLA Modules:
  0.0 631.9 jit_solution(259838609014529799)
XLA Ops:
  6.5 0.0 copy-start.2
  6.5 0.0 copy-start.1
  6.5 0.0 reduce-scatter.2.cloned.1.call-start
  6.5 6.4 %fusion.16 = (bf16[128,128,1]{2,1,0:T(8,128)(2,1)}, bf16[128,128,1]{2,1,0:T(8,128)(2,1)}) fusion(bf16[128,128,256]{2,1,0:T(8,128)(2,1)} %param.5), kind=kLoop, calls=%fused_computation.37 | loop fusion | bytes 131072 | tf_op jit(solution)/shard_map/slice | solution.py:72
  13.0 3.7 copy.15
  16.7 3.3 collective-permute-start.1
  20.0 3.7 copy.14
  23.7 3.5 collective-permute-start
  27.2 0.0 copy-done.2
  27.2 0.7 fusion.19
  27.9 0.0 copy-done.1
  27.9 0.7 fusion.17
  28.6 0.6 fusion.18
  29.2 0.0 collective-permute-done
  29.2 3.3 copy.12
  32.5 0.0 collective-permute-done.1
  32.5 3.3 copy.13
  35.8 11.0 %maximum_convert_fusion = f32[128,128,258]{2,1,0:T(8,128)S(1)} fusion(bf16[128,128,1]{2,1,0:T(8,128)(2,1)} %copy.13, bf16[128,128,256]{2,1,0:T(8,128)(2,1)} %param.5, bf16[128,128,1]{2,1,0:T(8,128)(2,1)} %copy.12), kind=kLoop, calls=%fused_computation.18 | loop fusion | flops 25362432 | bytes 25362432 | tf_op jit(solution)/shard_map/convert_element_type | solution.py:75
  46.7 0.0 copy-start
  46.8 9.1 %slice.160 = f32[128,128,256]{2,1,0:T(8,128)} slice(f32[128,128,258]{2,1,0:T(8,128)S(1)} %maximum_convert_fusion), slice={[0:128], [0:128], [1:257]} | slice | bytes 33554432 | tf_op jit(solution)/shard_map/slice | solution.py:33
  55.8 4.2 copy-done
  60.1 338.4 %multiply_reduce_fusion = (f32[128,256]{1,0:T(8,128)S(1)}, f32[128,128,256]{2,1,0:T(8,128)}) fusion(f32[]{:T(128)} %bitcast.37, f32[]{:T(128)} %bitcast.36, f32[]{:T(128)} %bitcast.35, f32[]{:T(128)} %bitcast.34, f32[]{:T(128)} %bitcast.33, f32[]{:T(128)} %bitcast.32, f32[]{:T(128)} %bitcast.31, f32[]{:T(128)} %bitcast.30, f32[128,128,256]{2,1,0:T(8,128)} %slice.160, ...), kind=kOutput, calls=%fused_computation.5 | output fusion | flops 1086291968 | bytes 84029440 | tf_op jit(solution)/shard_map/jit(cumsum)/reduce_window_sum | solution.py:52
  398.5 0.9 broadcast_subtract_fusion
  399.5 12.3 %all_gather.7 = f32[4,128,256]{2,1,0:T(8,128)S(1)} all-gather(f32[1,128,256]{2,1,0:T(8,128)S(1)} %get-tuple-element.108), channel_id=1, replica_groups=mesh['gx'=32,'gz'=4] {'gz'}, dimensions={0}, use_global_device_ids=true | all-gather | bytes 655360 | tf_op jit(solution)/shard_map/all_gather | solution.py:9
  411.8 0.2 while.14
  411.9 67.9 %multiply_reduce_fusion.1 = f32[128,256]{1,0:T(8,128)S(1)} fusion(f32[]{:T(128)} %bitcast.28, f32[]{:T(128)} %bitcast.27, f32[]{:T(128)} %bitcast.26, f32[]{:T(128)} %bitcast.25, f32[]{:T(128)} %bitcast.24, f32[]{:T(128)} %bitcast.23, f32[]{:T(128)} %bitcast.22, f32[]{:T(128)} %bitcast.21, f32[128,128,256]{2,1,0:T(8,128)} %slice.160, ...), kind=kLoop, calls=%fused_computation.6 | loop fusion | flops 352288768 | bytes 67240000 | tf_op jit(solution)/shard_map/reduce_sum | solution.py:55
  479.9 67.9 %multiply_reduce_fusion.2 = f32[128,256]{1,0:T(8,128)S(1)} fusion(f32[]{:T(128)} %bitcast.19, f32[]{:T(128)} %bitcast.18, f32[]{:T(128)} %bitcast.17, f32[]{:T(128)} %bitcast.16, f32[]{:T(128)} %bitcast.15, f32[]{:T(128)} %bitcast.14, f32[]{:T(128)} %bitcast.13, f32[]{:T(128)} %bitcast.12, f32[128,128,256]{2,1,0:T(8,128)} %slice.160, ...), kind=kLoop, calls=%fused_computation.7 | loop fusion | flops 352288768 | bytes 67240000 | tf_op jit(solution)/shard_map/reduce_sum | solution.py:55
  547.7 0.9 maximum_multiply_fusion
  548.6 0.0 reduce-scatter.2.cloned.1.call-update
  548.6 0.0 all-gather.2.cloned.1.call-start
  548.7 24.2 %reduce-scatter.2.cloned.1.call-done = f32[4,32,256]{2,1,0:T(8,128)} async-done(((f32[4,128,256]{2,1,0:T(8,128)}), f32[4,32,256]{2,1,0:T(8,128)}) %reduce-scatter.2.cloned.1.call-update) | async-done | bytes 131088 | tf_op jit(solution)/shard_map/reduce_scatter | solution.py:67
  572.8 1.5 convert_element_type.9
  574.4 0.0 all-gather.2.cloned.1.call-update
  574.4 47.4 %all-gather.2.cloned.1.call-done = bf16[4,32,8192]{2,1,0:T(8,128)(2,1)} async-done(((bf16[4,32,256]{2,1,0:T(8,128)(2,1)}), bf16[4,32,8192]{2,1,0:T(8,128)(2,1)}) %all-gather.2.cloned.1.call-update) | async-done | bytes 2097168 | tf_op jit(solution)/shard_map/all_gather | solution.py:78
  621.8 3.1 copy.23
  (4 shorter events, 0.1 us)
Async XLA Ops:
  6.5 20.7 %copy-start.2 = (f32[8]{0:T(128)S(1)}, f32[8]{0:T(128)}, u32[]{:S(2)}) copy-start(f32[8]{0:T(128)} %param.7) | copy-start | bytes 100
  6.5 21.4 %copy-start.1 = (f32[3,8]{1,0:T(4,128)S(1)}, f32[3,8]{1,0:T(4,128)}, u32[]{:S(2)}) copy-start(f32[3,8]{1,0:T(4,128)} %param.6) | copy-start | bytes 292
  6.5 566.3 %reduce-scatter.2.cloned.1.call-start = ((), (), s32[]{:S(2)}) async-start(), calls=%async_computation.1 | async-start | bytes 655360 | tf_op jit(solution)/shard_map/reduce_scatter | solution.py:67
  16.7 15.8 %collective-permute-start.1 = (bf16[1,128,128]{2,1,0:T(8,128)(2,1)S(1)}, bf16[1,128,128]{2,1,0:T(8,128)(2,1)S(1)}, u32[]{:S(2)}, u32[]{:S(2)}) collective-permute-start(bf16[1,128,128]{2,1,0:T(8,128)(2,1)S(1)} %bitcast.46), channel_id=1, source_target_pairs={{4,0},{8,4},{12,8},{16,12},{20,16},{24,20},{28,24},{32,28},{36,32}... | collective-permute-start | bytes 98312 | tf_op jit(solution)/shard_map/ppermute | solution.py:27
  23.7 5.5 collective-permute-start
  46.7 13.3 %copy-start = (f32[128,128,258]{2,1,0:T(8,128)}, f32[128,128,258]{2,1,0:T(8,128)S(1)}, u32[]{:S(2)}) copy-start(f32[128,128,258]{2,1,0:T(8,128)S(1)} %maximum_convert_fusion) | copy-start | bytes 50724868
  548.6 73.1 %all-gather.2.cloned.1.call-start = ((), (), s32[]{:S(2)}) async-start(), calls=%async_computation.2 | async-start | bytes 2162688 | tf_op jit(solution)/shard_map/all_gather | solution.py:78
Sparse Core Ops, SparseCore 0:
  548.7 24.0 reduce-scatter.1
  575.0 46.7 all-gather.1
where the time goes:
time: 642 us; the launch traced here: 632 us
  other arithmetic  489 us (76%)
  waiting for transfers between devices  71.6 us (11%)
  local copies, waits for them, and re-layouts  38.8 us (6%)
  between operations  13.7 us (2%)
  blocking collectives  12.3 us (2%)
  starting transfers between devices  6.9 us (1%)
    another operation x1, other arithmetic, brick_strip(): running = jnp.cumsum(optical, axis=0)  338 us
    reduce_sum x2, other arithmetic, brick_strip(): jnp.sum(lighted * colors[channel], axis=0)  136 us
    all_gather x1, waiting for transfers between devices, on_device(): return lax.all_gather(finished, 'gx', axis=2, tiled=True)  47.4 us
    reduce_scatter x1, waiting for transfers between devices, composite(): lax.psum_scatter(strips * ahead[None], 'gz', scatter_dimension=1, tiled=T...  24.2 us
    unnamed x9, local copies, waits for them, and re-layouts  14.7 us
  transfers between devices with their start and end apart: 4, of which 2 were waited for; matrix products, arithmetic and copies ran while one was open for 1% of the time, Pallas kernels for 0%

commit v1 on v0

v1 whole, which is shorter than its diff:
```python
import functools
import math

import jax
import jax.numpy as jnp
from jax import lax
from jax.experimental import pallas as pl
from jax.experimental.pallas import tpu as pltpu
from jax.sharding import PartitionSpec as P

F32, BF16 = jnp.float32, jnp.bfloat16
MESH = pl.DeviceIdType.MESH
RU = 16
ZB = 8
ROUNDS = 2
GATHER = lax.GatherDimensionNumbers(
    offset_dims=(),
    collapsed_slice_dims=(0,),
    start_index_map=(0,),
    operand_batching_dims=(1,),
    start_indices_batching_dims=(1,),
)


def look(table, index):
    return lax.gather(
        table, index[..., None], GATHER, (1, 1), mode=lax.GatherScatterMode.PROMISE_IN_BOUNDS
    )


def dot(a, b):
    return jnp.dot(a, b, preferred_element_type=F32)


def iota(shape, dim):
    return lax.broadcasted_iota(jnp.int32, shape, dim)


def tables(tfc, tfe, total_depth):
    knots = tfe.shape[0]
    row = iota((8, 128), 0)
    found = []
    for fn in range(4):
        scale = 0.4 if fn < 3 else -math.log2(math.e) / total_depth
        value = [(tfc[fn, k] if fn < 3 else tfe[k]) * scale for k in range(knots)]
        a = jnp.zeros((8, 128), F32)
        b = jnp.zeros((8, 128), F32)
        for k in range(knots):
            if k + 1 < knots:
                rise = value[k + 1] - value[k]
                a = jnp.where(row == k, value[k] - rise * float(k), a)
                b = jnp.where(row == k, rise * float(knots - 1), b)
            else:
                a = jnp.where(row == k, value[k], a)
        found += [a, b]
    return found


def kernel(
    total_depth, den, tfc, tfe, out,
    D, onehot, edge, halo_in, halo, W, A, E, tab, pb0, rb0, pb1, rb1, strip, bricks, blk,
    load_sem, halo_ssem, halo_rsem, strip_ssem, strip_rsem, own_sem,
    a_ssem, a_rsem, b_ssem, b_rsem, c_ssem, c_rsem,
):
    gx, gz = lax.axis_index("gx"), lax.axis_index("gz")
    n_gx, n_gz = lax.axis_size("gx"), lax.axis_size("gz")
    depth, rows, cols = den.shape
    core, chip_z, chip_x = lax.rem(gx, 2), lax.rem(gx // 2, 4), gx // 8
    NZB, NLOAD = depth // ZB, depth // ZB
    HALF = depth // 2

    def gx_of(x, z, c):
        return x * 8 + z * 2 + c

    loads = [
        pltpu.make_async_copy(
            den.at[k * ZB : (k + 1) * ZB], D.at[k * ZB : (k + 1) * ZB, RU : RU + rows, :], load_sem.at[k]
        )
        for k in range(NLOAD)
    ]
    for copy in loads:
        copy.start()

    left, right = lax.rem(gx + n_gx - 1, n_gx), lax.rem(gx + 1, n_gx)
    sibling = (gx_of(chip_x, chip_z, 1 - core), gz)
    z_peers = [(gx_of(chip_x, lax.rem(chip_z + k, 4), core), gz) for k in (1, 2, 3)]
    x_peers = [(gx_of(lax.rem(chip_x + k, 4), chip_z, core), gz) for k in (1, 2, 3)]
    y_peers = [(gx, lax.rem(gz + k, n_gz)) for k in (1, 2, 3)]
    barrier = pltpu.get_barrier_semaphore()
    peers = [(left, gz), (right, gz), sibling] + z_peers + x_peers + y_peers
    for peer in peers:
        pl.semaphore_signal(barrier, inc=1, device_id=peer, device_id_type=MESH)

    D[:, 0:RU, :] = jnp.zeros((depth, RU, cols), BF16)
    D[:, RU + rows : 2 * RU + rows, :] = jnp.zeros((depth, RU, cols), BF16)
    lane = lax.rem(iota((RU, 128), 1), HALF)

    def mark(z, _):
        onehot[z] = jnp.where(lane == z, 1.0, 0.0).astype(BF16)
        return 0

    lax.fori_loop(0, HALF, mark, 0)
    k, x = iota((cols, cols), 0), iota((cols, cols), 1)
    W[0:cols, :] = (jnp.where(k == x + 1, 1.0, 0.0) - jnp.where(k == x - 1, 1.0, 0.0)).astype(BF16)
    k, x = iota((128, cols), 0), iota((128, cols), 1)
    W[cols : cols + 128, :] = (
        jnp.where((k < HALF) & (x == cols - 1), 1.0, 0.0) - jnp.where((k >= HALF) & (x == 0), 1.0, 0.0)
    ).astype(BF16)
    k, x = iota((cols, 128), 0), iota((cols, 128), 1)
    E[...] = jnp.where(((k == 0) & (x < HALF)) | ((k == cols - 1) & (x >= HALF)), 1.0, 0.0).astype(BF16)
    m, k = iota((4 * RU, 12 * RU), 0), iota((4 * RU, 12 * RU), 1)
    at = (m // RU) * (3 * RU) + RU + lax.rem(m, RU)
    A[...] = (jnp.where(k == at + 1, 1.0, 0.0) - jnp.where(k == at - 1, 1.0, 0.0)).astype(BF16)
    for n, t in enumerate(tables(tfc, tfe, total_depth)):
        tab[n] = t

    lane_all = lax.rem(iota((rows, 128), 1), HALF)
    for part in range(2):
        acc = jnp.zeros((rows, 128), F32)
        for k in range(NLOAD // 2 * part, NLOAD // 2 * (part + 1)):
            loads[k].wait()
            spread = dot(D[k * ZB : (k + 1) * ZB, RU : RU + rows, :].reshape(ZB * rows, cols), E[...])
            for j in range(ZB):
                acc = jnp.where(lane_all == k * ZB + j - part * HALF, spread[j * rows : (j + 1) * rows], acc)
        edge[part] = acc.astype(BF16)

    pl.semaphore_wait(barrier, len(peers))
    halo_copies = [
        pltpu.make_async_remote_copy(
            src_ref=edge, dst_ref=halo_in.at[side], send_sem=halo_ssem.at[side], recv_sem=halo_rsem.at[side],
            device_id=(target, gz), device_id_type=MESH,
        )
        for side, target in ((0, left), (1, right))
    ]
    for copy in halo_copies:
        copy.start()
    for copy in halo_copies:
        copy.wait()
    lane_halo = iota((rows, 128), 1)
    keep_right = jnp.where(gx == n_gx - 1, 0.0, 1.0)
    keep_left = jnp.where(gx == 0, 0.0, 1.0)
    for part in range(2):
        halo[part] = jnp.where(
            lane_halo < HALF,
            halo_in[0, part].astype(F32) * keep_right,
            halo_in[1, part].astype(F32) * keep_left,
        ).astype(BF16)

    def unit_rows(u):
        return pl.multiple_of(lax.rem(gz + 1 + lax.rem(u, 4), 4) * (2 * RU) + (u // 4) * RU, RU)

    def slopes(y0, zb, pb, rb):
        z0 = pl.multiple_of(zb * ZB, ZB)
        block = D[pl.ds(z0, ZB), pl.ds(RU + y0, RU), :].reshape(ZB * RU, cols)
        part = z0 // HALF
        edges = halo[part, pl.ds(y0, RU), :][None] * onehot[pl.ds(z0 - part * HALF, ZB)]
        pb[...] = dot(jnp.concatenate([block, edges.reshape(ZB * RU, 128)], 1), W[...])
        for i in range(ZB // 4):
            near = D[pl.ds(z0 + 4 * i, 4), pl.ds(y0, 3 * RU), :].reshape(12 * RU, cols)
            rb[4 * RU * i : 4 * RU * (i + 1), :] = dot(A[...], near)

    def march(y0, zb, pb, rb, carry):
        z0 = zb * ZB
        T = [tab[n] for n in range(8)]

        def step(z, carry):
            r0 = pl.multiple_of(z * RU, RU)
            dx, dy = pb[pl.ds(r0, RU)], rb[pl.ds(r0, RU)]
            dens = D[z0 + z, pl.ds(RU + y0, RU), :].astype(F32)
            new = []
            for k in range(4):
                i, j = k // 2, k % 2
                sl = (slice(8 * i, 8 * i + 8), slice(128 * j, 128 * j + 128))
                p, r, d = dx[sl], dy[sl], dens[sl]
                run, clear, red, green, blue = carry[5 * k : 5 * k + 5]
                q = (0.75 * p + r) * lax.rsqrt((p * p + 0.0625) + r * r)
                ix = (d * 7.0).astype(jnp.int32)
                run = (run + look(T[6], ix)) + look(T[7], ix) * d
                after = jnp.exp2(run)
                w = (clear - after) * (1.25 + q)
                red = red + w * (look(T[0], ix) + look(T[1], ix) * d)
                green = green + w * (look(T[2], ix) + look(T[3], ix) * d)
                blue = blue + w * (look(T[4], ix) + look(T[5], ix) * d)
                new += [run, after, red, green, blue]
            return tuple(new)

        return lax.fori_loop(0, ZB, step, carry, unroll=True)

    def strip_copy(u):
        slot = u // 4
        target = lax.rem(gz + 1 + lax.rem(u, 4), 4)
        return pltpu.make_async_remote_copy(
            src_ref=strip.at[u], dst_ref=bricks.at[slot, gz], send_sem=strip_ssem.at[u],
            recv_sem=strip_rsem.at[slot, gz], device_id=(gx, target), device_id_type=MESH,
        )

    def column(x, z):
        return pl.multiple_of(gx_of(x, z, core) * cols, cols)

    def place(h, p, x, z):
        return out.at[2 * p : 2 * p + 2, RU * h : RU * h + RU, pl.ds(column(x, z), cols)]

    def own_copy(h):
        return pltpu.make_async_copy(
            blk.at[h], out.at[:, RU * h : RU * h + RU, pl.ds(column(chip_x, chip_z), cols)], own_sem.at[h]
        )

    def a_copies(h):
        found = []
        for p, targets, me in ((0, z_peers, chip_z), (1, x_peers, chip_x)):
            for k, target in enumerate(targets):
                found.append(
                    pltpu.make_async_remote_copy(
                        src_ref=blk.at[h, 2 * p : 2 * p + 2], dst_ref=place(h, p, chip_x, chip_z),
                        send_sem=a_ssem.at[h, p, k], recv_sem=a_rsem.at[h, p, k],
                        device_id=target, device_id_type=MESH,
                    )
                )
        return found

    def b_copy(h, p, k, n, spot):
        return pltpu.make_async_remote_copy(
            src_ref=spot, dst_ref=spot, send_sem=b_ssem.at[h, p, k, n], recv_sem=b_rsem.at[h, p, k, n],
            device_id=(x_peers, z_peers)[p][k], device_id_type=MESH,
        )

    def b_copies(h):
        return [
            b_copy(h, p, k, n, place(h, p, n, chip_z) if p else place(h, p, chip_x, n))
            for p in range(2) for k in range(3) for n in range(4)
        ]

    def a_arrivals(h):
        found = []
        for p in range(2):
            for k in range(3):
                back = 3 - k
                x = lax.rem(chip_x + back, 4) if p else chip_x
                z = chip_z if p else lax.rem(chip_z + back, 4)
                spot = place(h, p, x, z)
                found.append(
                    pltpu.make_async_remote_copy(
                        src_ref=spot, dst_ref=spot, send_sem=a_ssem.at[h, p, k], recv_sem=a_rsem.at[h, p, k],
                        device_id=(z_peers, x_peers)[p][k], device_id_type=MESH,
                    )
                )
        return found

    def b_arrivals(h):
        found = []
        for k in range(3):
            x, z = lax.rem(chip_x + 3 - k, 4), lax.rem(chip_z + 3 - k, 4)
            for n in range(4):
                found += [b_copy(h, 0, k, n, place(h, 0, x, n)), b_copy(h, 1, k, n, place(h, 1, n, z))]
        return found

    def c_copies(h, c):
        found = []
        for chip in range(16):
            at = pl.multiple_of((2 * chip + c) * cols, cols)
            spot = out.at[:, RU * h : RU * h + RU, pl.ds(at, cols)]
            found.append(
                pltpu.make_async_remote_copy(
                    src_ref=spot, dst_ref=spot, send_sem=c_ssem.at[h, chip], recv_sem=c_rsem.at[h, chip],
                    device_id=sibling, device_id_type=MESH,
                )
            )
        return found

    def composite(h):
        for k in (1, 2, 3):
            brick = lax.rem(gz + k, 4)
            pltpu.make_async_remote_copy(
                src_ref=strip.at[0], dst_ref=bricks.at[h, brick], send_sem=strip_ssem.at[0],
                recv_sem=strip_rsem.at[h, brick], device_id=(gx, brick), device_id_type=MESH,
            ).wait_recv()
        ahead = bricks[h, 0, 3]
        total = [bricks[h, 0, c] for c in range(3)] + [1.0 - ahead]
        for b in range(1, 4):
            through = bricks[h, b, 3]
            total = [total[c] + ahead * bricks[h, b, c] for c in range(3)] + [total[3] + ahead * (1.0 - through)]
            ahead = ahead * through
        for c in range(4):
            blk[h, c] = total[c].astype(BF16)
        own_copy(h).start()
        for copy in a_copies(h):
            copy.start()

    def stage_b(h):
        own_copy(h).wait()
        for copy in a_arrivals(h):
            copy.wait_recv()
        for copy in b_copies(h):
            copy.start()

    def stage_c(h):
        for copy in b_arrivals(h):
            copy.wait_recv()
        for copy in c_copies(h, core):
            copy.start()

    def unit(u, _):
        y0 = unit_rows(u)
        zero, one = jnp.zeros((8, 128), F32), jnp.ones((8, 128), F32)
        slopes(y0, 0, pb0, rb0)

        def pair(i, carry):
            slopes(y0, 2 * i + 1, pb1, rb1)
            carry = march(y0, 2 * i, pb0, rb0, carry)
            slopes(y0, lax.rem(2 * i + 2, NZB), pb0, rb0)
            return march(y0, 2 * i + 1, pb1, rb1, carry)

        carry = lax.fori_loop(0, NZB // 2, pair, (zero, one, zero, zero, zero) * 4)

        def keep(ref):
            for k in range(4):
                i, j = k // 2, k % 2
                _, clear, red, green, blue = carry[5 * k : 5 * k + 5]
                for c, v in enumerate((red, green, blue, clear)):
                    ref[c, 8 * i : 8 * i + 8, 128 * j : 128 * j + 128] = v

        @pl.when(lax.rem(u, 4) < 3)
        def _():
            keep(strip.at[u])
            strip_copy(u).start()

        @pl.when(lax.rem(u, 4) == 3)
        def _():
            keep(bricks.at[u // 4, gz])

        @pl.when(u == 4)
        def _():
            composite(0)

        @pl.when(u == 5)
        def _():
            stage_b(0)

        @pl.when(u == 6)
        def _():
            stage_c(0)

        return 0

    lax.fori_loop(0, 4 * ROUNDS, unit, 0)
    composite(1)
    stage_b(1)
    stage_c(1)
    for h in range(ROUNDS):
        for copy in c_copies(h, 1 - core):
            copy.wait_recv()
        for copy in a_copies(h) + b_copies(h) + c_copies(h, core):
            copy.wait_send()
        for s in range(3):
            strip_copy(4 * h + s).wait_send()


def render(density, tf_color, tf_extinction):
    depth, rows, cols = density.shape
    n_gx, n_gz = lax.axis_size("gx"), lax.axis_size("gz")
    D = pltpu.SemaphoreType.DMA
    return pl.pallas_call(
        functools.partial(kernel, depth * n_gz),
        out_shape=jax.ShapeDtypeStruct((4, rows // n_gz, cols * n_gx), BF16),
        in_specs=[
            pl.BlockSpec(memory_space=pl.ANY),
            pl.BlockSpec(memory_space=pltpu.SMEM),
            pl.BlockSpec(memory_space=pltpu.SMEM),
        ],
        out_specs=pl.BlockSpec(memory_space=pl.ANY),
        scratch_shapes=[
            pltpu.VMEM((depth, rows + 2 * RU, cols), BF16),
            pltpu.VMEM((depth // 2, RU, 128), BF16),
            pltpu.VMEM((2, rows, 128), BF16),
            pltpu.VMEM((2, 2, rows, 128), BF16),
            pltpu.VMEM((2, rows, 128), BF16),
            pltpu.VMEM((cols + 128, cols), BF16),
            pltpu.VMEM((4 * RU, 12 * RU), BF16),
            pltpu.VMEM((cols, 128), BF16),
            pltpu.VMEM((8, 8, 128), F32),
            pltpu.VMEM((ZB * RU, cols), F32),
            pltpu.VMEM((ZB * RU, cols), F32),
            pltpu.VMEM((ZB * RU, cols), F32),
            pltpu.VMEM((ZB * RU, cols), F32),
            pltpu.VMEM((4 * ROUNDS, 4, RU, cols), F32),
            pltpu.VMEM((ROUNDS, 4, 4, RU, cols), F32),
            pltpu.VMEM((ROUNDS, 4, RU, cols), BF16),
            D((depth // ZB,)),
            D((2,)),
            D((2,)),
            D((4 * ROUNDS,)),
            D((ROUNDS, 4)),
            D((ROUNDS,)),
            D((ROUNDS, 2, 3)),
            D((ROUNDS, 2, 3)),
            D((ROUNDS, 2, 3, 4)),
            D((ROUNDS, 2, 3, 4)),
            D((ROUNDS, 16)),
            D((ROUNDS, 16)),
        ],
        compiler_params=pltpu.CompilerParams(
            collective_id=0, has_side_effects=True, vmem_limit_bytes=58 * 2**20
        ),
    )(density, tf_color, tf_extinction)


def solution(mesh):
    in_specs = (P("gz", None, "gx"), P(), P())
    return jax.shard_map(
        render, mesh=mesh, in_specs=in_specs, out_specs=P(None, "gz", None), check_vma=False
    )
```

time: 642 us -> 67.7 us (0.11); the launches traced: 632 us -> 67.5 us
  other arithmetic: 489 us -> 0 us
  waiting for transfers between devices: 71.6 us -> 0 us
  Pallas kernels: 0 us -> 64.4 us
  local copies, waits for them, and re-layouts: 38.8 us -> 3.1 us
  between operations: 13.7 us -> 0.01 us
  blocking collectives: 12.3 us -> 0 us
  starting transfers between devices: 6.9 us -> 0 us
    another operation x1 -> x0, other arithmetic: 338 us -> none  [brick_strip(): running = jnp.cumsum(optical, axis=0)]
    reduce_sum x2 -> x0, other arithmetic: 136 us -> none  [brick_strip(): jnp.sum(lighted * colors[channel], axis=0)]
    pallas_call x0 -> x1, Pallas kernels: none -> 64.4 us  [render(): pl.pallas_call(functools.partial(kernel, depth * n_gz), out_shape=jax.Sha...]
    all_gather x1 -> x0, waiting for transfers between devices: 47.4 us -> none  [on_device(): return lax.all_gather(finished, 'gx', axis=2, tiled=True)]
    reduce_scatter x1 -> x0, waiting for transfers between devices: 24.2 us -> none  [composite(): lax.psum_scatter(strips * ahead[None], 'gz', scatter_dimension=1, tiled=T...]
    slice x5 -> x0, local copies, waits for them, and re-layouts: 17.5 us -> none  [the longest x1 9.09 us: shade_and_color(): middle = block[:, :, 1:-1]]
    convert_element_type x2 -> x0, other arithmetic: 12.5 us -> none  [the longest x1 11 us: on_device(): padded.astype(jnp.float32)]
    all_gather x1 -> x0, blocking collectives: 12.3 us -> none  [carried_in(): pieces = lax.all_gather(value, axis)]
  transfers between devices with their start and end apart: 4 -> 0, of which waited for: 2 -> 0; matrix products, arithmetic and copies ran while one was open for 1% -> 0% of each run, Pallas kernels for 0% -> 0%
where the time goes in v1:
time: 67.7 us; the launch traced here: 67.5 us
  Pallas kernels  64.4 us (95%)
  local copies, waits for them, and re-layouts  3.1 us (5%)
    pallas_call x1, Pallas kernels, render(): pl.pallas_call(functools.partial(kernel, depth * n_gz), out_shape=jax.Sha...  64.4 us
    unnamed x1, local copies, waits for them, and re-layouts  3.1 us

profile of v1, /device:TPU:1, one launch (start us, length us, event | category | flops | bytes accessed | tf_op | source)
XLA Modules:
  0.0 67.5 jit_solution(7533354189014447673)
XLA Ops:
  0.0 64.4 %shard_map.37 = bf16[4,32,8192]{2,1,0:T(8,128)(2,1)} custom-call(bf16[128,128,256]{2,1,0:T(8,128)(2,1)} %den.1, f32[3,8]{1,0:T(4,128)} %tfc.1, f32[8]{0:T(128)} %tfe.1), custom_call_target="tpu_custom_call" | custom-call | tf_op jit(solution)/shard_map/pallas_call | solution.py:362
  64.4 3.1 %copy.5 = bf16[4,32,8192]{2,1,0:T(8,128)(2,1)} copy(bf16[4,32,8192]{2,1,0:T(8,128)(2,1)} %shard_map.37) | data formatting | bytes 4194304

commit v2 on v1

--- a/solution.py
+++ b/solution.py
@@ -11,6 +11,7 @@
 F32, BF16 = jnp.float32, jnp.bfloat16
 MESH = pl.DeviceIdType.MESH
 RU = 16
+AHEAD = 4
 ZB = 8
 ROUNDS = 2
 GATHER = lax.GatherDimensionNumbers(
@@ -49,7 +50,7 @@
             if k + 1 < knots:
                 rise = value[k + 1] - value[k]
                 a = jnp.where(row == k, value[k] - rise * float(k), a)
-                b = jnp.where(row == k, rise * float(knots - 1), b)
+                b = jnp.where(row == k, rise, b)
             else:
                 a = jnp.where(row == k, value[k], a)
         found += [a, b]
@@ -58,7 +59,7 @@
 
 def kernel(
     total_depth, den, tfc, tfe, out,
-    D, onehot, edge, halo_in, halo, W, A, E, tab, pb0, rb0, pb1, rb1, strip, bricks, blk,
+    D, onehot, edge, halo_in, halo, W, A, E, tab, pb, rb, strip, bricks, blk,
     load_sem, halo_ssem, halo_rsem, strip_ssem, strip_rsem, own_sem,
     a_ssem, a_rsem, b_ssem, b_rsem, c_ssem, c_rsem,
 ):
@@ -101,11 +102,14 @@
 
     lax.fori_loop(0, HALF, mark, 0)
     k, x = iota((cols, cols), 0), iota((cols, cols), 1)
-    W[0:cols, :] = (jnp.where(k == x + 1, 1.0, 0.0) - jnp.where(k == x - 1, 1.0, 0.0)).astype(BF16)
+    diff = jnp.where(k == x + 1, 1.0, 0.0) - jnp.where(k == x - 1, 1.0, 0.0)
+    W[0:cols, 0:cols] = diff.astype(BF16)
+    W[0:cols, cols : 2 * cols] = (0.75 * diff).astype(BF16)
+    W[0:cols, 2 * cols : 3 * cols] = jnp.where(k == x, 7.0, 0.0).astype(BF16)
     k, x = iota((128, cols), 0), iota((128, cols), 1)
-    W[cols : cols + 128, :] = (
-        jnp.where((k < HALF) & (x == cols - 1), 1.0, 0.0) - jnp.where((k >= HALF) & (x == 0), 1.0, 0.0)
-    ).astype(BF16)
+    diff = jnp.where((k < HALF) & (x == cols - 1), 1.0, 0.0) - jnp.where((k >= HALF) & (x == 0), 1.0, 0.0)
+    W[cols : cols + 128, 0:cols] = diff.astype(BF16)
+    W[cols : cols + 128, cols : 2 * cols] = (0.75 * diff).astype(BF16)
     k, x = iota((cols, 128), 0), iota((cols, 128), 1)
     E[...] = jnp.where(((k == 0) & (x < HALF)) | ((k == cols - 1) & (x >= HALF)), 1.0, 0.0).astype(BF16)
     m, k = iota((4 * RU, 12 * RU), 0), iota((4 * RU, 12 * RU), 1)
@@ -154,7 +158,10 @@
         block = D[pl.ds(z0, ZB), pl.ds(RU + y0, RU), :].reshape(ZB * RU, cols)
         part = z0 // HALF
         edges = halo[part, pl.ds(y0, RU), :][None] * onehot[pl.ds(z0 - part * HALF, ZB)]
-        pb[...] = dot(jnp.concatenate([block, edges.reshape(ZB * RU, 128)], 1), W[...])
+        lhs = jnp.concatenate([block, edges.reshape(ZB * RU, 128)], 1)
+        pb[0] = dot(lhs, W[:, 0:cols])
+        pb[1] = dot(lhs, W[:, cols : 2 * cols])
+        pb[2] = dot(block, W[0:cols, 2 * cols : 3 * cols])
         for i in range(ZB // 4):
             near = D[pl.ds(z0 + 4 * i, 4), pl.ds(y0, 3 * RU), :].reshape(12 * RU, cols)
             rb[4 * RU * i : 4 * RU * (i + 1), :] = dot(A[...], near)
@@ -165,16 +172,16 @@
 
         def step(z, carry):
             r0 = pl.multiple_of(z * RU, RU)
-            dx, dy = pb[pl.ds(r0, RU)], rb[pl.ds(r0, RU)]
-            dens = D[z0 + z, pl.ds(RU + y0, RU), :].astype(F32)
+            dx, dx75, dens = [pb[n, pl.ds(r0, RU)] for n in range(3)]
+            dy = rb[pl.ds(r0, RU)]
             new = []
             for k in range(4):
                 i, j = k // 2, k % 2
                 sl = (slice(8 * i, 8 * i + 8), slice(128 * j, 128 * j + 128))
-                p, r, d = dx[sl], dy[sl], dens[sl]
+                p, p75, r, d = dx[sl], dx75[sl], dy[sl], dens[sl]
                 run, clear, red, green, blue = carry[5 * k : 5 * k + 5]
-                q = (0.75 * p + r) * lax.rsqrt((p * p + 0.0625) + r * r)
-                ix = (d * 7.0).astype(jnp.int32)
+                q = (p75 + r) * lax.rsqrt((p * p + 0.0625) + r * r)
+                ix = d.astype(jnp.int32)
                 run = (run + look(T[6], ix)) + look(T[7], ix) * d
                 after = jnp.exp2(run)
                 w = (clear - after) * (1.25 + q)
@@ -302,15 +309,16 @@
     def unit(u, _):
         y0 = unit_rows(u)
         zero, one = jnp.zeros((8, 128), F32), jnp.ones((8, 128), F32)
-        slopes(y0, 0, pb0, rb0)
-
-        def pair(i, carry):
-            slopes(y0, 2 * i + 1, pb1, rb1)
-            carry = march(y0, 2 * i, pb0, rb0, carry)
-            slopes(y0, lax.rem(2 * i + 2, NZB), pb0, rb0)
-            return march(y0, 2 * i + 1, pb1, rb1, carry)
-
-        carry = lax.fori_loop(0, NZB // 2, pair, (zero, one, zero, zero, zero) * 4)
+
+        def blocks(i, carry):
+            for n in range(AHEAD):
+                carry = march(y0, AHEAD * i + n, pb.at[n], rb.at[n], carry)
+                ahead = AHEAD * (i + 1) + n
+                later = jnp.minimum(u + ahead // NZB, 4 * ROUNDS - 1)
+                slopes(unit_rows(later), lax.rem(ahead, NZB), pb.at[n], rb.at[n])
+            return carry
+
+        carry = lax.fori_loop(0, NZB // AHEAD, blocks, (zero, one, zero, zero, zero) * 4)
 
         def keep(ref):
             for k in range(4):
@@ -342,6 +350,8 @@
 
         return 0
 
+    for n in range(AHEAD):
+        slopes(unit_rows(0), n, pb.at[n], rb.at[n])
     lax.fori_loop(0, 4 * ROUNDS, unit, 0)
     composite(1)
     stage_b(1)
@@ -374,14 +384,12 @@
             pltpu.VMEM((2, rows, 128), BF16),
             pltpu.VMEM((2, 2, rows, 128), BF16),
             pltpu.VMEM((2, rows, 128), BF16),
-            pltpu.VMEM((cols + 128, cols), BF16),
+            pltpu.VMEM((cols + 128, 3 * cols), BF16),
             pltpu.VMEM((4 * RU, 12 * RU), BF16),
             pltpu.VMEM((cols, 128), BF16),
             pltpu.VMEM((8, 8, 128), F32),
-            pltpu.VMEM((ZB * RU, cols), F32),
-            pltpu.VMEM((ZB * RU, cols), F32),
-            pltpu.VMEM((ZB * RU, cols), F32),
-            pltpu.VMEM((ZB * RU, cols), F32),
+            pltpu.VMEM((AHEAD, 3, ZB * RU, cols), F32),
+            pltpu.VMEM((AHEAD, ZB * RU, cols), F32),
             pltpu.VMEM((4 * ROUNDS, 4, RU, cols), F32),
             pltpu.VMEM((ROUNDS, 4, 4, RU, cols), F32),
             pltpu.VMEM((ROUNDS, 4, RU, cols), BF16),

time: 67.7 us -> 64.9 us (0.959)
  Pallas kernels: 64.4 us -> 61.6 us
    pallas_call x1, Pallas kernels: 64.4 us -> 61.6 us  [render(): pl.pallas_call(functools.partial(kernel, depth * n_gz), out_shape=jax.Sha...]
where the time goes in v2:
time: 64.9 us; the launch traced here: 64.7 us
  Pallas kernels  61.6 us (95%)
  local copies, waits for them, and re-layouts  3.1 us (5%)
    pallas_call x1, Pallas kernels, render(): pl.pallas_call(functools.partial(kernel, depth * n_gz), out_shape=jax.Sha...  61.6 us
    unnamed x1, local copies, waits for them, and re-layouts  3.1 us

profile of v2, /device:TPU:1, one launch (start us, length us, event | category | flops | bytes accessed | tf_op | source)
XLA Modules:
  0.0 64.7 jit_solution(13280973798669619502)
XLA Ops:
  0.0 61.6 %shard_map.37 = bf16[4,32,8192]{2,1,0:T(8,128)(2,1)} custom-call(bf16[128,128,256]{2,1,0:T(8,128)(2,1)} %den.1, f32[3,8]{1,0:T(4,128)} %tfc.1, f32[8]{0:T(128)} %tfe.1), custom_call_target="tpu_custom_call" | custom-call | tf_op jit(solution)/shard_map/pallas_call | solution.py:372
  61.6 3.1 %copy.5 = bf16[4,32,8192]{2,1,0:T(8,128)(2,1)} copy(bf16[4,32,8192]{2,1,0:T(8,128)(2,1)} %shard_map.37) | data formatting | bytes 4194304

commit v3 on v2

v3 whole, which is shorter than its diff:
```python
import functools
import math

import jax
import jax.numpy as jnp
from jax import lax
from jax.experimental import pallas as pl
from jax.experimental.pallas import tpu as pltpu
from jax.sharding import PartitionSpec as P

F32, BF16 = jnp.float32, jnp.bfloat16
MESH = pl.DeviceIdType.MESH
RU = 16
AHEAD = 4
ZB = 8
ROUNDS = 2
UNITS = 4 * ROUNDS
GATHER = lax.GatherDimensionNumbers(
    offset_dims=(),
    collapsed_slice_dims=(0,),
    start_index_map=(0,),
    operand_batching_dims=(1,),
    start_indices_batching_dims=(1,),
)


def look(table, index):
    return lax.gather(
        table, index[..., None], GATHER, (1, 1), mode=lax.GatherScatterMode.PROMISE_IN_BOUNDS
    )


def dot(a, b):
    return jnp.dot(a, b, preferred_element_type=F32)


def iota(shape, dim):
    return lax.broadcasted_iota(jnp.int32, shape, dim)


def tables(tf, total_depth):
    knots = tf.shape[1]
    row = iota((8, 128), 0)
    found = []
    for fn in range(4):
        scale = 0.4 if fn < 3 else -math.log2(math.e) / total_depth
        value = [tf[fn, k] * scale for k in range(knots)]
        a = jnp.zeros((8, 128), F32)
        b = jnp.zeros((8, 128), F32)
        for k in range(knots):
            if k + 1 < knots:
                rise = value[k + 1] - value[k]
                a = jnp.where(row == k, value[k] - rise * float(k), a)
                b = jnp.where(row == k, rise, b)
            else:
                a = jnp.where(row == k, value[k], a)
        found += [a, b]
    return found


def kernel(
    total_depth, den, tf, out,
    D, onehot, edge, halo_in, halo, W, A, E, tab, pb, rb, strip, bricks, blk,
    load_sem, halo_ssem, halo_rsem, strip_ssem, strip_rsem, own_sem,
    a_ssem, a_rsem, b_ssem, b_rsem, c_ssem, c_rsem,
):
    gx, gz = lax.axis_index("gx"), lax.axis_index("gz")
    n_gx, n_gz = lax.axis_size("gx"), lax.axis_size("gz")
    depth, rows, cols = den.shape
    core, chip_z, chip_x = lax.rem(gx, 2), lax.rem(gx // 2, 4), gx // 8
    NZB = depth // ZB
    HALF = depth // 2

    def gx_of(x, z, c):
        return x * 8 + z * 2 + c

    def unit_rows(u):
        return pl.multiple_of(lax.rem(gz + 1 + lax.rem(u, 4), 4) * (2 * RU) + (u // 4) * RU, RU)

    def load(u):
        y0 = unit_rows(u)
        return pltpu.make_async_copy(
            den.at[:, pl.ds(y0, RU), :], D.at[:, pl.ds(RU + y0, RU), :], load_sem.at[u]
        )

    def begin_load(u, _):
        load(u).start()
        return 0

    lax.fori_loop(0, UNITS, begin_load, 0)

    left, right = lax.rem(gx + n_gx - 1, n_gx), lax.rem(gx + 1, n_gx)
    sibling = (gx_of(chip_x, chip_z, 1 - core), gz)
    z_peers = [(gx_of(chip_x, lax.rem(chip_z + k, 4), core), gz) for k in (1, 2, 3)]
    x_peers = [(gx_of(lax.rem(chip_x + k, 4), chip_z, core), gz) for k in (1, 2, 3)]
    y_peers = [(gx, lax.rem(gz + k, n_gz)) for k in (1, 2, 3)]
    barrier = pltpu.get_barrier_semaphore()
    peers = [(left, gz), (right, gz), sibling] + z_peers + x_peers + y_peers
    for peer in peers:
        pl.semaphore_signal(barrier, inc=1, device_id=peer, device_id_type=MESH)

    D[:, 0:RU, :] = jnp.zeros((depth, RU, cols), BF16)
    D[:, RU + rows : 2 * RU + rows, :] = jnp.zeros((depth, RU, cols), BF16)
    lane = lax.rem(iota((RU, 128), 1), HALF)

    def mark(z, _):
        onehot[z] = jnp.where(lane == z, 1.0, 0.0).astype(BF16)
        return 0

    lax.fori_loop(0, HALF, mark, 0)
    k, x = iota((cols, cols), 0), iota((cols, cols), 1)
    diff = jnp.where(k == x + 1, 1.0, 0.0) - jnp.where(k == x - 1, 1.0, 0.0)
    W[0:cols, 0:cols] = diff.astype(BF16)
    W[0:cols, cols : 2 * cols] = (0.75 * diff).astype(BF16)
    W[0:cols, 2 * cols : 3 * cols] = jnp.where(k == x, 7.0, 0.0).astype(BF16)
    k, x = iota((128, cols), 0), iota((128, cols), 1)
    diff = jnp.where((k < HALF) & (x == cols - 1), 1.0, 0.0) - jnp.where((k >= HALF) & (x == 0), 1.0, 0.0)
    W[cols : cols + 128, 0:cols] = diff.astype(BF16)
    W[cols : cols + 128, cols : 2 * cols] = (0.75 * diff).astype(BF16)
    k, x = iota((cols, 128), 0), iota((cols, 128), 1)
    E[...] = jnp.where(((k == 0) & (x < HALF)) | ((k == cols - 1) & (x >= HALF)), 1.0, 0.0).astype(BF16)
    m, k = iota((4 * RU, 12 * RU), 0), iota((4 * RU, 12 * RU), 1)
    at = (m // RU) * (3 * RU) + RU + lax.rem(m, RU)
    A[...] = (jnp.where(k == at + 1, 1.0, 0.0) - jnp.where(k == at - 1, 1.0, 0.0)).astype(BF16)
    for n, t in enumerate(tables(tf, total_depth)):
        tab[n] = t

    lane_half = lax.rem(iota((RU, 128), 1), HALF)
    lane_halo = iota((RU, 128), 1)
    keep_right = jnp.where(gx == n_gx - 1, 0.0, 1.0)
    keep_left = jnp.where(gx == 0, 0.0, 1.0)

    def extract(u):
        load(u).wait()
        y0 = unit_rows(u)
        for part in range(2):
            block = D[part * HALF : (part + 1) * HALF, pl.ds(RU + y0, RU), :].reshape(HALF * RU, cols)
            spread = dot(block, E[...])
            acc = jnp.zeros((RU, 128), F32)
            for z in range(HALF):
                acc = jnp.where(lane_half == z, spread[z * RU : (z + 1) * RU], acc)
            edge[u, part] = acc.astype(BF16)

    def halo_copies(u):
        return [
            pltpu.make_async_remote_copy(
                src_ref=edge.at[u], dst_ref=halo_in.at[side, u], send_sem=halo_ssem.at[side, u],
                recv_sem=halo_rsem.at[side, u], device_id=(target, gz), device_id_type=MESH,
            )
            for side, target in ((0, left), (1, right))
        ]

    def halo_arrive(u):
        for copy in halo_copies(u):
            copy.wait()
        for part in range(2):
            halo[u, part] = jnp.where(
                lane_halo < HALF,
                halo_in[0, u, part].astype(F32) * keep_right,
                halo_in[1, u, part].astype(F32) * keep_left,
            ).astype(BF16)

    extract(0)
    pl.semaphore_wait(barrier, len(peers))
    for copy in halo_copies(0):
        copy.start()

    def send_edges(u, _):
        extract(u)
        for copy in halo_copies(u):
            copy.start()
        return 0

    lax.fori_loop(1, UNITS, send_edges, 0)
    halo_arrive(0)

    def slopes(u, zb, pb, rb):
        y0 = unit_rows(u)
        z0 = pl.multiple_of(zb * ZB, ZB)
        block = D[pl.ds(z0, ZB), pl.ds(RU + y0, RU), :].reshape(ZB * RU, cols)
        part = z0 // HALF
        edges = halo[u, part][None] * onehot[pl.ds(z0 - part * HALF, ZB)]
        lhs = jnp.concatenate([block, edges.reshape(ZB * RU, 128)], 1)
        pb[0] = dot(lhs, W[:, 0:cols])
        pb[1] = dot(lhs, W[:, cols : 2 * cols])
        pb[2] = dot(block, W[0:cols, 2 * cols : 3 * cols])
        for i in range(ZB // 4):
            near = D[pl.ds(z0 + 4 * i, 4), pl.ds(y0, 3 * RU), :].reshape(12 * RU, cols)
            rb[4 * RU * i : 4 * RU * (i + 1), :] = dot(A[...], near)

    def march(y0, zb, pb, rb, carry):
        z0 = zb * ZB
        T = [tab[n] for n in range(8)]

        def step(z, carry):
            r0 = pl.multiple_of(z * RU, RU)
            dx, dx75, dens = [pb[n, pl.ds(r0, RU)] for n in range(3)]
            dy = rb[pl.ds(r0, RU)]
            new = []
            for k in range(4):
                i, j = k // 2, k % 2
                sl = (slice(8 * i, 8 * i + 8), slice(128 * j, 128 * j + 128))
                p, p75, r, d = dx[sl], dx75[sl], dy[sl], dens[sl]
                run, clear, red, green, blue = carry[5 * k : 5 * k + 5]
                q = (p75 + r) * lax.rsqrt((p * p + 0.0625) + r * r)
                ix = d.astype(jnp.int32)
                run = (run + look(T[6], ix)) + look(T[7], ix) * d
                after = jnp.exp2(run)
                w = (clear - after) * (1.25 + q)
                red = red + w * (look(T[0], ix) + look(T[1], ix) * d)
                green = green + w * (look(T[2], ix) + look(T[3], ix) * d)
                blue = blue + w * (look(T[4], ix) + look(T[5], ix) * d)
                new += [run, after, red, green, blue]
            return tuple(new)

        return lax.fori_loop(0, ZB, step, carry, unroll=True)

    def strip_copy(u):
        slot = u // 4
        target = lax.rem(gz + 1 + lax.rem(u, 4), 4)
        return pltpu.make_async_remote_copy(
            src_ref=strip.at[u], dst_ref=bricks.at[slot, gz], send_sem=strip_ssem.at[u],
            recv_sem=strip_rsem.at[slot, gz], device_id=(gx, target), device_id_type=MESH,
        )

    first, second = (z_peers, x_peers), (x_peers, z_peers)

    def place(h, p, k, j, c):
        x, z = lax.rem(chip_x + (j if p else k), 4), lax.rem(chip_z + (k if p else j), 4)
        at = pl.multiple_of(gx_of(x, z, c) * cols, cols)
        return out.at[2 * p : 2 * p + 2, RU * h : RU * h + RU, pl.ds(at, cols)]

    def own_copy(h):
        at = pl.multiple_of(gx * cols, cols)
        return pltpu.make_async_copy(blk.at[h], out.at[:, RU * h : RU * h + RU, pl.ds(at, cols)], own_sem.at[h])

    def held(h, p, k, j):
        return blk.at[h, 2 * p : 2 * p + 2] if k == 0 and j == 0 else place(h, p, k, j, core)

    def send(src, dst, ssem, rsem, target):
        return pltpu.make_async_remote_copy(
            src_ref=src, dst_ref=dst, send_sem=ssem, recv_sem=rsem, device_id=target, device_id_type=MESH
        )

    def a_copy(h, p, m):
        return send(held(h, p, 0, 0), place(h, p, 0, 0, core), a_ssem.at[h, p, m - 1], a_rsem.at[h, p, m - 1], first[p][m - 1])

    def a_arrival(h, p, j):
        spot = place(h, p, 0, j, core)
        return send(spot, spot, a_ssem.at[h, p, 3 - j], a_rsem.at[h, p, 3 - j], first[p][3 - j])

    def b_copy(h, p, m, j):
        return send(held(h, p, 0, j), place(h, p, 0, j, core), b_ssem.at[h, p, m - 1, j], b_rsem.at[h, p, m - 1, j], second[p][m - 1])

    def b_arrival(h, p, k, j):
        spot = place(h, p, k, j, core)
        return send(spot, spot, b_ssem.at[h, p, 3 - k, j], b_rsem.at[h, p, 3 - k, j], second[p][3 - k])

    def c_copy(h, p, k, j):
        return send(held(h, p, k, j), place(h, p, k, j, core), c_ssem.at[h, p, k, j], c_rsem.at[h, p, k, j], sibling)

    def c_arrival(h, p, k, j):
        spot = place(h, p, k, j, 1 - core)
        return send(spot, spot, c_ssem.at[h, p, k, j], c_rsem.at[h, p, k, j], sibling)

    NEAR = (1, 3, 2)

    def composite(h):
        for k in (1, 2, 3):
            brick = lax.rem(gz + k, 4)
            pltpu.make_async_remote_copy(
                src_ref=strip.at[0], dst_ref=bricks.at[h, brick], send_sem=strip_ssem.at[0],
                recv_sem=strip_rsem.at[h, brick], device_id=(gx, brick), device_id_type=MESH,
            ).wait_recv()
        ahead = bricks[h, 0, 3]
        total = [bricks[h, 0, c] for c in range(3)] + [1.0 - ahead]
        for b in range(1, 4):
            through = bricks[h, b, 3]
            total = [total[c] + ahead * bricks[h, b, c] for c in range(3)] + [total[3] + ahead * (1.0 - through)]
            ahead = ahead * through
        for c in range(4):
            blk[h, c] = total[c].astype(BF16)
        for p in range(2):
            for m in NEAR:
                a_copy(h, p, m).start()
        for p in range(2):
            for m in NEAR:
                b_copy(h, p, m, 0).start()
        own_copy(h).start()
        for p in range(2):
            c_copy(h, p, 0, 0).start()

    def stage_b(h):
        own_copy(h).wait()
        for j in NEAR:
            for p in range(2):
                a_arrival(h, p, j).wait_recv()
                for m in NEAR:
                    b_copy(h, p, m, j).start()
                c_copy(h, p, 0, j).start()

    def stage_c(h):
        for j in (0,) + NEAR:
            for k in NEAR:
                for p in range(2):
                    b_arrival(h, p, k, j).wait_recv()
                    c_copy(h, p, k, j).start()

    def unit(u, _):
        y0 = unit_rows(u)
        zero, one = jnp.zeros((8, 128), F32), jnp.ones((8, 128), F32)

        def blocks(i, carry):
            @pl.when((i == NZB // AHEAD - 2) & (u < UNITS - 1))
            def _():
                halo_arrive(u + 1)

            for n in range(AHEAD):
                carry = march(y0, AHEAD * i + n, pb.at[n], rb.at[n], carry)
                ahead = AHEAD * (i + 1) + n
                later = jnp.minimum(u + ahead // NZB, UNITS - 1)
                slopes(later, lax.rem(ahead, NZB), pb.at[n], rb.at[n])
            return carry

        carry = lax.fori_loop(0, NZB // AHEAD, blocks, (zero, one, zero, zero, zero) * 4)

        def keep(ref):
            for k in range(4):
                i, j = k // 2, k % 2
                _, clear, red, green, blue = carry[5 * k : 5 * k + 5]
                for c, v in enumerate((red, green, blue, clear)):
                    ref[c, 8 * i : 8 * i + 8, 128 * j : 128 * j + 128] = v

        @pl.when(lax.rem(u, 4) < 3)
        def _():
            keep(strip.at[u])
            strip_copy(u).start()

        @pl.when(lax.rem(u, 4) == 3)
        def _():
            keep(bricks.at[u // 4, gz])

        @pl.when(u == 4)
        def _():
            composite(0)

        @pl.when(u == 5)
        def _():
            stage_b(0)

        @pl.when(u == 6)
        def _():
            stage_c(0)

        return 0

    for n in range(AHEAD):
        slopes(0, n, pb.at[n], rb.at[n])
    lax.fori_loop(0, UNITS, unit, 0)
    composite(1)
    stage_b(1)
    stage_c(1)
    for h in range(ROUNDS):
        for p in range(2):
            for j in range(4):
                for k in range(4):
                    c_arrival(h, p, k, j).wait_recv()
                    c_copy(h, p, k, j).wait_send()
                    if k:
                        b_copy(h, p, k, j).wait_send()
                if j:
                    a_copy(h, p, j).wait_send()
        for i in range(3):
            strip_copy(4 * h + i).wait_send()


def render(density, tf_color, tf_extinction):
    depth, rows, cols = density.shape
    n_gx, n_gz = lax.axis_size("gx"), lax.axis_size("gz")
    D = pltpu.SemaphoreType.DMA
    return pl.pallas_call(
        functools.partial(kernel, depth * n_gz),
        out_shape=jax.ShapeDtypeStruct((4, rows // n_gz, cols * n_gx), BF16),
        in_specs=[
            pl.BlockSpec(memory_space=pl.ANY),
            pl.BlockSpec(memory_space=pltpu.SMEM),
        ],
        out_specs=pl.BlockSpec(memory_space=pl.ANY),
        scratch_shapes=[
            pltpu.VMEM((depth, rows + 2 * RU, cols), BF16),
            pltpu.VMEM((depth // 2, RU, 128), BF16),
            pltpu.VMEM((UNITS, 2, RU, 128), BF16),
            pltpu.VMEM((2, UNITS, 2, RU, 128), BF16),
            pltpu.VMEM((UNITS, 2, RU, 128), BF16),
            pltpu.VMEM((cols + 128, 3 * cols), BF16),
            pltpu.VMEM((4 * RU, 12 * RU), BF16),
            pltpu.VMEM((cols, 128), BF16),
            pltpu.VMEM((8, 8, 128), F32),
            pltpu.VMEM((AHEAD, 3, ZB * RU, cols), F32),
            pltpu.VMEM((AHEAD, ZB * RU, cols), F32),
            pltpu.VMEM((4 * ROUNDS, 4, RU, cols), F32),
            pltpu.VMEM((ROUNDS, 4, 4, RU, cols), F32),
            pltpu.VMEM((ROUNDS, 4, RU, cols), BF16),
            D((UNITS,)),
            D((2, UNITS)),
            D((2, UNITS)),
            D((UNITS,)),
            D((ROUNDS, 4)),
            D((ROUNDS,)),
            D((ROUNDS, 2, 3)),
            D((ROUNDS, 2, 3)),
            D((ROUNDS, 2, 3, 4)),
            D((ROUNDS, 2, 3, 4)),
            D((ROUNDS, 2, 4, 4)),
            D((ROUNDS, 2, 4, 4)),
        ],
        compiler_params=pltpu.CompilerParams(
            collective_id=0, has_side_effects=True, vmem_limit_bytes=50 * 2**20
        ),
    )(density, jnp.concatenate([tf_color, tf_extinction[None]], 0))


def solution(mesh):
    in_specs = (P("gz", None, "gx"), P(), P())
    return jax.shard_map(
        render, mesh=mesh, in_specs=in_specs, out_specs=P(None, "gz", None), check_vma=False
    )
```

time: 64.9 us -> 56.1 us (0.86)
  Pallas kernels: 61.6 us -> 53.9 us
  local copies, waits for them, and re-layouts: 3.1 us -> 1.32 us
  other arithmetic: 0 us -> 0.71 us
    pallas_call x1, Pallas kernels: 61.6 us -> 53.9 us  [render(): pl.pallas_call(functools.partial(kernel, depth * n_gz), out_shape=jax.Sha...]
    unnamed x1, local copies, waits for them, and re-layouts: 3.1 us -> 1.32 us
    concatenate x0 -> x1, other arithmetic: none -> 0.71 us  [render(): jnp.concatenate([tf_color, tf_extinction[None]], 0)]
where the time goes in v3:
time: 56.1 us; the launch traced here: 56 us
  Pallas kernels  53.9 us (96%)
  local copies, waits for them, and re-layouts  1.32 us (2%)
  other arithmetic  0.71 us (1%)
    pallas_call x1, Pallas kernels, render(): pl.pallas_call(functools.partial(kernel, depth * n_gz), out_shape=jax.Sha...  53.9 us
    unnamed x1, local copies, waits for them, and re-layouts  1.32 us

profile of v3, /device:TPU:1, one launch (start us, length us, event | category | flops | bytes accessed | tf_op | source)
XLA Modules:
  0.0 56.0 jit_solution(3582024702812920591)
XLA Ops:
  0.0 0.7 %pad_maximum_fusion.tf = f32[4,8]{1,0:T(4,128)S(1)} fusion(f32[1,8]{1,0:T(1,128)} %bitcast.1, f32[3,8]{1,0:T(4,128)} %param.4), kind=kLoop, calls=%fused_computation | loop fusion | flops 32 | bytes 256 | tf_op jit(solution)/shard_map/concatenate | solution.py:420
  0.7 53.9 %shard_map.37 = bf16[4,32,8192]{2,1,0:T(8,128)(2,1)S(1)} custom-call(bf16[128,128,256]{2,1,0:T(8,128)(2,1)} %den.1, f32[4,8]{1,0:T(4,128)S(1)} %pad_maximum_fusion.tf), custom_call_target="tpu_custom_call" | custom-call | tf_op jit(solution)/shard_map/pallas_call | solution.py:381
  54.6 1.3 %copy.5 = bf16[4,32,8192]{2,1,0:T(8,128)(2,1)} copy(bf16[4,32,8192]{2,1,0:T(8,128)(2,1)S(1)} %shard_map.37) | data formatting | bytes 4194304

commit v4 on v3

--- a/solution.py
+++ b/solution.py
@@ -11,7 +11,7 @@
 F32, BF16 = jnp.float32, jnp.bfloat16
 MESH = pl.DeviceIdType.MESH
 RU = 16
-AHEAD = 4
+AHEAD = 8
 ZB = 8
 ROUNDS = 2
 UNITS = 4 * ROUNDS
@@ -111,12 +111,10 @@
     k, x = iota((cols, cols), 0), iota((cols, cols), 1)
     diff = jnp.where(k == x + 1, 1.0, 0.0) - jnp.where(k == x - 1, 1.0, 0.0)
     W[0:cols, 0:cols] = diff.astype(BF16)
-    W[0:cols, cols : 2 * cols] = (0.75 * diff).astype(BF16)
-    W[0:cols, 2 * cols : 3 * cols] = jnp.where(k == x, 7.0, 0.0).astype(BF16)
+    W[0:cols, cols : 2 * cols] = jnp.where(k == x, 7.0, 0.0).astype(BF16)
     k, x = iota((128, cols), 0), iota((128, cols), 1)
     diff = jnp.where((k < HALF) & (x == cols - 1), 1.0, 0.0) - jnp.where((k >= HALF) & (x == 0), 1.0, 0.0)
     W[cols : cols + 128, 0:cols] = diff.astype(BF16)
-    W[cols : cols + 128, cols : 2 * cols] = (0.75 * diff).astype(BF16)
     k, x = iota((cols, 128), 0), iota((cols, 128), 1)
     E[...] = jnp.where(((k == 0) & (x < HALF)) | ((k == cols - 1) & (x >= HALF)), 1.0, 0.0).astype(BF16)
     m, k = iota((4 * RU, 12 * RU), 0), iota((4 * RU, 12 * RU), 1)
@@ -182,8 +180,7 @@
         edges = halo[u, part][None] * onehot[pl.ds(z0 - part * HALF, ZB)]
         lhs = jnp.concatenate([block, edges.reshape(ZB * RU, 128)], 1)
         pb[0] = dot(lhs, W[:, 0:cols])
-        pb[1] = dot(lhs, W[:, cols : 2 * cols])
-        pb[2] = dot(block, W[0:cols, 2 * cols : 3 * cols])
+        pb[1] = dot(block, W[0:cols, cols : 2 * cols])
         for i in range(ZB // 4):
             near = D[pl.ds(z0 + 4 * i, 4), pl.ds(y0, 3 * RU), :].reshape(12 * RU, cols)
             rb[4 * RU * i : 4 * RU * (i + 1), :] = dot(A[...], near)
@@ -194,15 +191,15 @@
 
         def step(z, carry):
             r0 = pl.multiple_of(z * RU, RU)
-            dx, dx75, dens = [pb[n, pl.ds(r0, RU)] for n in range(3)]
+            dx, dens = [pb[n, pl.ds(r0, RU)] for n in range(2)]
             dy = rb[pl.ds(r0, RU)]
             new = []
             for k in range(4):
                 i, j = k // 2, k % 2
                 sl = (slice(8 * i, 8 * i + 8), slice(128 * j, 128 * j + 128))
-                p, p75, r, d = dx[sl], dx75[sl], dy[sl], dens[sl]
+                p, r, d = dx[sl], dy[sl], dens[sl]
                 run, clear, red, green, blue = carry[5 * k : 5 * k + 5]
-                q = (p75 + r) * lax.rsqrt((p * p + 0.0625) + r * r)
+                q = (0.75 * p + r) * lax.rsqrt((p * p + 0.0625) + r * r)
                 ix = d.astype(jnp.int32)
                 run = (run + look(T[6], ix)) + look(T[7], ix) * d
                 after = jnp.exp2(run)
@@ -357,21 +354,29 @@
     for n in range(AHEAD):
         slopes(0, n, pb.at[n], rb.at[n])
     lax.fori_loop(0, UNITS, unit, 0)
-    composite(1)
-    stage_b(1)
-    stage_c(1)
-    for h in range(ROUNDS):
+    def finish(h):
         for p in range(2):
             for j in range(4):
                 for k in range(4):
                     c_arrival(h, p, k, j).wait_recv()
                     c_copy(h, p, k, j).wait_send()
-                    if k:
-                        b_copy(h, p, k, j).wait_send()
-                if j:
-                    a_copy(h, p, j).wait_send()
+
+    def sent(h):
+        for p in range(2):
+            for m in range(1, 4):
+                for j in range(4):
+                    b_copy(h, p, m, j).wait_send()
+                a_copy(h, p, m).wait_send()
         for i in range(3):
             strip_copy(4 * h + i).wait_send()
+
+    composite(1)
+    finish(0)
+    stage_b(1)
+    sent(0)
+    stage_c(1)
+    sent(1)
+    finish(1)
 
 
 def render(density, tf_color, tf_extinction):
@@ -392,11 +397,11 @@
             pltpu.VMEM((UNITS, 2, RU, 128), BF16),
             pltpu.VMEM((2, UNITS, 2, RU, 128), BF16),
             pltpu.VMEM((UNITS, 2, RU, 128), BF16),
-            pltpu.VMEM((cols + 128, 3 * cols), BF16),
+            pltpu.VMEM((cols + 128, 2 * cols), BF16),
             pltpu.VMEM((4 * RU, 12 * RU), BF16),
             pltpu.VMEM((cols, 128), BF16),
             pltpu.VMEM((8, 8, 128), F32),
-            pltpu.VMEM((AHEAD, 3, ZB * RU, cols), F32),
+            pltpu.VMEM((AHEAD, 2, ZB * RU, cols), F32),
             pltpu.VMEM((AHEAD, ZB * RU, cols), F32),
             pltpu.VMEM((4 * ROUNDS, 4, RU, cols), F32),
             pltpu.VMEM((ROUNDS, 4, 4, RU, cols), F32),

time: 56.1 us -> 55.2 us (0.984)
  Pallas kernels: 53.9 us -> 53.1 us
    pallas_call x1, Pallas kernels: 53.9 us -> 53.1 us  [render(): pl.pallas_call(functools.partial(kernel, depth * n_gz), out_shape=jax.Sha...]
where the time goes in v4:
time: 55.2 us; the launch traced here: 55.1 us
  Pallas kernels  53.1 us (96%)
  local copies, waits for them, and re-layouts  1.32 us (2%)
  other arithmetic  0.71 us (1%)
    pallas_call x1, Pallas kernels, render(): pl.pallas_call(functools.partial(kernel, depth * n_gz), out_shape=jax.Sha...  53.1 us
    unnamed x1, local copies, waits for them, and re-layouts  1.32 us

profile of v4, /device:TPU:1, one launch (start us, length us, event | category | flops | bytes accessed | tf_op | source)
XLA Modules:
  0.0 55.1 jit_solution(14214051117730126385)
XLA Ops:
  0.0 0.7 %pad_maximum_fusion.tf = f32[4,8]{1,0:T(4,128)S(1)} fusion(f32[1,8]{1,0:T(1,128)} %bitcast.1, f32[3,8]{1,0:T(4,128)} %param.4), kind=kLoop, calls=%fused_computation | loop fusion | flops 32 | bytes 256 | tf_op jit(solution)/shard_map/concatenate | solution.py:425
  0.7 53.1 %shard_map.37 = bf16[4,32,8192]{2,1,0:T(8,128)(2,1)S(1)} custom-call(bf16[128,128,256]{2,1,0:T(8,128)(2,1)} %den.1, f32[4,8]{1,0:T(4,128)S(1)} %pad_maximum_fusion.tf), custom_call_target="tpu_custom_call" | custom-call | tf_op jit(solution)/shard_map/pallas_call | solution.py:386
  53.8 1.3 %copy.5 = bf16[4,32,8192]{2,1,0:T(8,128)(2,1)} copy(bf16[4,32,8192]{2,1,0:T(8,128)(2,1)S(1)} %shard_map.37) | data formatting | bytes 4194304

commit v5 on v4

--- a/solution.py
+++ b/solution.py
@@ -189,19 +189,18 @@
         z0 = zb * ZB
         T = [tab[n] for n in range(8)]
 
-        def step(z, carry):
-            r0 = pl.multiple_of(z * RU, RU)
-            dx, dens = [pb[n, pl.ds(r0, RU)] for n in range(2)]
-            dy = rb[pl.ds(r0, RU)]
+        def step(i, z, carry):
+            r0 = pl.multiple_of(z * RU + 8 * i, 8)
+            dx, dens = [pb[n, pl.ds(r0, 8)] for n in range(2)]
+            dy = rb[pl.ds(r0, 8)]
             new = []
-            for k in range(4):
-                i, j = k // 2, k % 2
-                sl = (slice(8 * i, 8 * i + 8), slice(128 * j, 128 * j + 128))
+            for j in range(2):
+                sl = (slice(0, 8), slice(128 * j, 128 * j + 128))
                 p, r, d = dx[sl], dy[sl], dens[sl]
-                run, clear, red, green, blue = carry[5 * k : 5 * k + 5]
-                q = (0.75 * p + r) * lax.rsqrt((p * p + 0.0625) + r * r)
+                run, clear, red, green, blue = carry[5 * j : 5 * j + 5]
+                q = (0.75 * p + r) * lax.rsqrt(p * p + (r * r + 0.0625))
                 ix = d.astype(jnp.int32)
-                run = (run + look(T[6], ix)) + look(T[7], ix) * d
+                run = run + (look(T[6], ix) + look(T[7], ix) * d)
                 after = jnp.exp2(run)
                 w = (clear - after) * (1.25 + q)
                 red = red + w * (look(T[0], ix) + look(T[1], ix) * d)
@@ -210,7 +209,10 @@
                 new += [run, after, red, green, blue]
             return tuple(new)
 
-        return lax.fori_loop(0, ZB, step, carry, unroll=True)
+        halves = []
+        for i in range(2):
+            halves += lax.fori_loop(0, ZB, functools.partial(step, i), carry[10 * i : 10 * i + 10], unroll=True)
+        return tuple(halves)
 
     def strip_copy(u):
         slot = u // 4

time: 55.2 us -> 55.1 us (level)
  no operation moved by 1% of the time
where the time goes in v5:
time: 55.1 us; the launch traced here: 55 us
  Pallas kernels  52.9 us (96%)
  local copies, waits for them, and re-layouts  1.32 us (2%)
  other arithmetic  0.71 us (1%)
    pallas_call x1, Pallas kernels, render(): pl.pallas_call(functools.partial(kernel, depth * n_gz), out_shape=jax.Sha...  52.9 us
    unnamed x1, local copies, waits for them, and re-layouts  1.32 us

profile of v5, /device:TPU:1, one launch (start us, length us, event | category | flops | bytes accessed | tf_op | source)
XLA Modules:
  0.0 55.0 jit_solution(12344934804848999408)
XLA Ops:
  0.0 0.7 %pad_maximum_fusion.tf = f32[4,8]{1,0:T(4,128)S(1)} fusion(f32[1,8]{1,0:T(1,128)} %bitcast.1, f32[3,8]{1,0:T(4,128)} %param.4), kind=kLoop, calls=%fused_computation | loop fusion | flops 32 | bytes 256 | tf_op jit(solution)/shard_map/concatenate | solution.py:427
  0.7 52.9 %shard_map.37 = bf16[4,32,8192]{2,1,0:T(8,128)(2,1)S(1)} custom-call(bf16[128,128,256]{2,1,0:T(8,128)(2,1)} %den.1, f32[4,8]{1,0:T(4,128)S(1)} %pad_maximum_fusion.tf), custom_call_target="tpu_custom_call" | custom-call | tf_op jit(solution)/shard_map/pallas_call | solution.py:388
  53.7 1.3 %copy.5 = bf16[4,32,8192]{2,1,0:T(8,128)(2,1)} copy(bf16[4,32,8192]{2,1,0:T(8,128)(2,1)S(1)} %shard_map.37) | data formatting | bytes 4194304

commit v6 on v5

--- a/solution.py
+++ b/solution.py
@@ -87,7 +87,7 @@
         load(u).start()
         return 0
 
-    lax.fori_loop(0, UNITS, begin_load, 0)
+    load(0).start()
 
     left, right = lax.rem(gx + n_gx - 1, n_gx), lax.rem(gx + 1, n_gx)
     sibling = (gx_of(chip_x, chip_z, 1 - core), gz)
@@ -98,6 +98,7 @@
     peers = [(left, gz), (right, gz), sibling] + z_peers + x_peers + y_peers
     for peer in peers:
         pl.semaphore_signal(barrier, inc=1, device_id=peer, device_id_type=MESH)
+    lax.fori_loop(1, UNITS, begin_load, 0)
 
     D[:, 0:RU, :] = jnp.zeros((depth, RU, cols), BF16)
     D[:, RU + rows : 2 * RU + rows, :] = jnp.zeros((depth, RU, cols), BF16)

time: 55.1 us -> 55 us (level)
  no operation moved by 1% of the time
where the time goes in v6:
time: 55 us; the launch traced here: 54.8 us
  Pallas kernels  52.8 us (96%)
  local copies, waits for them, and re-layouts  1.32 us (2%)
  other arithmetic  0.71 us (1%)
    pallas_call x1, Pallas kernels, render(): pl.pallas_call(functools.partial(kernel, depth * n_gz), out_shape=jax.Sha...  52.8 us
    unnamed x1, local copies, waits for them, and re-layouts  1.32 us

profile of v6, /device:TPU:1, one launch (start us, length us, event | category | flops | bytes accessed | tf_op | source)
XLA Modules:
  0.0 54.8 jit_solution(2847675816697823734)
XLA Ops:
  0.0 0.7 %pad_maximum_fusion.tf = f32[4,8]{1,0:T(4,128)S(1)} fusion(f32[1,8]{1,0:T(1,128)} %bitcast.1, f32[3,8]{1,0:T(4,128)} %param.4), kind=kLoop, calls=%fused_computation | loop fusion | flops 32 | bytes 256 | tf_op jit(solution)/shard_map/concatenate | solution.py:428
  0.7 52.8 %shard_map.37 = bf16[4,32,8192]{2,1,0:T(8,128)(2,1)S(1)} custom-call(bf16[128,128,256]{2,1,0:T(8,128)(2,1)} %den.1, f32[4,8]{1,0:T(4,128)S(1)} %pad_maximum_fusion.tf), custom_call_target="tpu_custom_call" | custom-call | tf_op jit(solution)/shard_map/pallas_call | solution.py:389
  53.5 1.3 %copy.5 = bf16[4,32,8192]{2,1,0:T(8,128)(2,1)} copy(bf16[4,32,8192]{2,1,0:T(8,128)(2,1)S(1)} %shard_map.37) | data formatting | bytes 4194304
